TPU v7x, 32 devices: a whole 2x2x4 slice. The times are simulated.
32 devices in a mesh: groups: 2 (over x), arc: 2 (over core), blk: 8 (over z, y).
Axes of the slice: x: 2, y: 2, z: 4, core: 2. Of those that a mesh axis runs over, the one named last changes fastest.
Arguments:
- queries: bfloat16 [6144, 640], P(('groups', 'arc', 'blk')), parts along dimension 0, may hold values from -128 to 128
- keys: bfloat16 [6144, 640], P(('groups', 'arc', 'blk')), parts along dimension 0, may hold values from -4 to 4
- values: bfloat16 [6144, 640], P(('groups', 'arc', 'blk')), parts along dimension 0, may hold values from -6 to 6
- out_weight: bfloat16 [640, 1024], replicated, may hold values from -0.25 to 0.25
- covis: int32 [192, 96], P('groups'), parts along dimension 0, may hold values from 0 to 1, as said below
- block_view: int32 [192], P('groups'), parts along dimension 0, may hold values from 0 to 95, each once
Outputs:
- projected: bfloat16 [6144, 1024], P(('groups', 'arc', 'blk')), parts along dimension 0
There are 2 independent parts, one for each index of `groups`. A program takes and returns all parts, laid end to end along the dimension named above; an argument that names none is the same for every part. Nothing has to cross between parts.
Inputs may be any that keep to these rules, and one draw needn't show every extreme that they name: `covis`: symmetric, with ones on the diagonal. `block_view`: each view once.
All inputs are finite; a program needn't handle non-finite values.
Results may differ from a plain program's by a relative error of at most 0.008.
Values may be sent and summed in bfloat16 or wider, within the bound.
A program may use at most 128 MiB of HBM per device.

v0:
```python
import jax
import jax.numpy as jnp
from jax import lax
from jax.sharding import PartitionSpec as P

HEADS = 10
HD = 64
BLOCK = 32


NEG = -1e30
HIGH = lax.Precision.HIGHEST


def block_table(covis, block_view):
    count = covis.shape[0]
    slots = (block_view[:, None] == jnp.arange(count, dtype=jnp.int32)[None, :]).astype(jnp.float32)
    linked = jnp.dot(slots, covis.astype(jnp.float32), precision=HIGH)
    return jnp.dot(linked, slots.T, precision=HIGH)


def select_rows(table, wanted):
    count = table.shape[0]
    picks = (wanted[:, None] == jnp.arange(count, dtype=jnp.int32)[None, :]).astype(jnp.float32)
    return jnp.dot(picks, table, precision=HIGH)


def start_state(rows):
    return (
        jnp.zeros((rows, HEADS * HD), jnp.float32),
        jnp.full((rows, HEADS), NEG, jnp.float32),
        jnp.zeros((rows, HEADS), jnp.float32),
    )


def seen_blocks(qvis, offset, length):
    count = qvis.shape[1]
    kblock = (offset + jnp.arange(length, dtype=jnp.int32)) // BLOCK
    konehot = (kblock[:, None] == jnp.arange(count, dtype=jnp.int32)[None, :]).astype(jnp.float32)
    return jnp.dot(qvis, konehot.T, precision=HIGH)


def attend_slice(state, qrows, seen, kpart, vpart):
    acc, most, total = state
    rows = qrows.shape[0]
    length = kpart.shape[0]
    keep = (jnp.repeat(seen, BLOCK, axis=0) > 0.5)[:, None, :]
    q3 = qrows.reshape(rows, HEADS, HD)
    k3 = kpart.reshape(length, HEADS, HD)
    v3 = vpart.reshape(length, HEADS, HD)
    scores = jnp.einsum("qhd,nhd->qhn", q3, k3, preferred_element_type=jnp.float32) * HD ** (-0.5)
    scores = jnp.where(keep, scores, NEG)
    fresh = jnp.maximum(most, jnp.max(scores, axis=-1))
    probs = jnp.where(keep, jnp.exp(scores - fresh[..., None]), 0.0)
    factor = jnp.exp(most - fresh)
    total = total * factor + jnp.sum(probs, axis=-1)
    mixed = jnp.einsum(
        "qhn,nhd->qhd", probs.astype(jnp.bfloat16), v3, preferred_element_type=jnp.float32
    )
    acc = acc.reshape(rows, HEADS, HD) * factor[..., None] + mixed
    return (acc.reshape(rows, HEADS * HD), fresh, total)


def make_fold(qrows, qvis):

    def fold(state, pieces, start):
        kpart, vpart = pieces
        length = kpart.shape[0]
        width = kpart.shape[1]
        step = 512
        kslices = kpart.reshape(length // step, step, width)
        vslices = vpart.reshape(length // step, step, width)
        offsets = step * jnp.arange(length // step, dtype=jnp.int32)

        def inner(carry, item):
            kslice, vslice, offset = item
            seen = seen_blocks(qvis, offset, step)
            carry = attend_slice(carry, qrows, seen, kslice, vslice)
            return (carry, None)

        result, _ = lax.scan(inner, state, (kslices, vslices, offsets))
        return result

    return fold


def finish(acc, total, out_weight):
    rows = acc.shape[0]
    attn = (
        (acc.reshape(rows, HEADS, HD) / total[..., None])
        .reshape(rows, HEADS * HD)
        .astype(jnp.bfloat16)
    )
    return jnp.dot(attn, out_weight, preferred_element_type=jnp.float32).astype(jnp.bfloat16)


def body(queries, keys, values, out_weight, covis, block_view):
    tok = queries.shape[0]
    per = tok // BLOCK
    n_blk = lax.axis_size("blk")
    arc_at = lax.axis_index("arc")
    blk_at = lax.axis_index("blk")
    table = block_table(covis, block_view)
    local = jnp.arange(per, dtype=jnp.int32)
    wanted = (arc_at * n_blk + blk_at) * per + local
    qvis = select_rows(table, wanted)
    fold = make_fold(queries, qvis)
    acc, most, total = fold(
        start_state(tok),
        (
            lax.all_gather(keys, ("arc", "blk"), axis=0, tiled=True),
            lax.all_gather(values, ("arc", "blk"), axis=0, tiled=True),
        ),
        jnp.int32(0),
    )
    return finish(acc, total, out_weight)


def solution(mesh):
    return jax.shard_map(
        body,
        mesh=mesh,
        in_specs=(
            P(("groups", "arc", "blk"), None),
            P(("groups", "arc", "blk"), None),
            P(("groups", "arc", "blk"), None),
            P(),
            P("groups", None),
            P("groups"),
        ),
        out_specs=P(("groups", "arc", "blk"), None),
        check_vma=False,
    )
```

profile of v0, /device:TPU:0, one launch (start us, length us, event | category | flops | bytes accessed | tf_op | source)
XLA Modules:
  0.0 209.8 jit_solution(13912486632489403978)
XLA Ops:
  6.5 0.7 all-gather.3.cloned.1.call-update
  7.3 0.7 all-gather.5.cloned.1.call-update
  8.0 1.8 copy.9
  9.9 1.0 fusion.22
  10.9 0.9 fusion.24
  12.0 49.1 %all-gather.3.cloned.1.call-done = bf16[3072,640]{1,0:T(8,128)(2,1)} async-done(((bf16[192,640]{1,0:T(8,128)(2,1)}), bf16[3072,640]{1,0:T(8,128)(2,1)}) %all-gather.3.cloned.1.call-update) | async-done | bytes 3932176 | tf_op jit(solution)/shard_map/all_gather | solution.py:111
  61.1 50.1 %all-gather.5.cloned.1.call-done = bf16[3072,640]{1,0:T(8,128)(2,1)} async-done(((bf16[192,640]{1,0:T(8,128)(2,1)}), bf16[3072,640]{1,0:T(8,128)(2,1)}) %all-gather.5.cloned.1.call-update) | async-done | bytes 3932176 | tf_op jit(solution)/shard_map/all_gather | solution.py:112
  111.2 0.9 broadcast_in_dim.53
  112.1 88.5 %while.17 = (s32[]{:T(128)}, f32[192,640]{0,1:T(8,128)}, f32[192,10]{0,1:T(8,128)S(1)}, f32[192,10]{0,1:T(8,128)S(1)}, s32[6]{0:T(128)S(1)}, /*index=5*/f32[6,96...) while((s32[]{:T(128)}, f32[192,640]{0,1:T(8,128)}, ...), condition=%wide.region_3.4_spmd.clone, body=%wide.region_0.3_spmd.clone.sunk | while | flops 268292480 | bytes 24039876 | solution.py:81
  112.1 0.6 dynamic_slice.28
  112.7 0.6 add_select_fusion.2
  113.2 0.3 fusion.52
  113.6 1.4 constant_dynamic-slice_fusion.3
  115.0 0.3 copy.16
  115.3 3.8 %fusion.53 = (f32[192,10]{0,1:T(8,128)S(1)}, f32[10,512,192]{1,2,0:T(8,128)}) fusion(pred[192,512]{1,0:T(8,128)(4,1)S(1)} %bitcast.75, bf16[512,10,64]{0,2,1:T(8,128)(2,1)S(1)} %bitcast.74, bf16[192,10,64]{0,2,1:T(8,128)(2,1)} %bitcast.79), kind=kOutput, calls=%fused_computation.2.clone.1 | convolution fusion | flops 128776320 | bytes 4939264 | tf_op jit(solution)/shard_map/while/body/eval_jaxpr/qhd,nhd->qhn/dot_general | solution.py:51
  119.0 3.4 %fusion.54 = f32[192,10]{0,1:T(8,128)S(1)} fusion(f32[10,512,192]{1,2,0:T(8,128)} %get-tuple-element.257, f32[192,10]{0,1:T(8,128)S(1)} %select_maximum_fusion.2, pred[192,512]{1,0:T(8,128)(4,1)S(1)} %bitcast.76), kind=kLoop, calls=%fused_computation.3.clone.1 | loop fusion | flops 4913280 | bytes 4045824 | tf_op jit(solution)/shard_map/while/body/eval_jaxpr/reduce_sum | solution.py:56
  122.7 3.3 %fusion.56 = f32[192,10,64]{0,2,1:T(8,128)S(1)} fusion(bf16[512,10,64]{0,2,1:T(8,128)(2,1)S(1)} %bitcast.78, f32[10,512,192]{1,2,0:T(8,128)} %get-tuple-element.257, f32[192,10]{0,1:T(8,128)S(1)} %select_maximum_fusion.2, pred[192,512]{1,0:T(8,128)(4,1)S(1)} %bitcast.77, f32[192,10,64]{0,2,1:T(8,128)S(1)} %bitcast.82, ...), kind=kOutput, calls=%fused_computation.8.clone.1 | convolution fusion | flops 130990080 | bytes 5684224 | tf_op jit(solution)/shard_map/while/body/eval_jaxpr/qhn,nhd->qhd/dot_general | solution.py:57
  126.0 0.8 copy-done.2
  126.9 0.6 dynamic_slice.28
  127.4 0.6 add_select_fusion.2
  128.0 0.3 fusion.52
  128.3 1.4 constant_dynamic-slice_fusion.3
  130.0 3.8 %fusion.53 = (f32[192,10]{0,1:T(8,128)S(1)}, f32[10,512,192]{1,2,0:T(8,128)}) fusion(pred[192,512]{1,0:T(8,128)(4,1)S(1)} %bitcast.75, bf16[512,10,64]{0,2,1:T(8,128)(2,1)S(1)} %bitcast.74, bf16[192,10,64]{0,2,1:T(8,128)(2,1)} %bitcast.79), kind=kOutput, calls=%fused_computation.2.clone.1 | convolution fusion | flops 128776320 | bytes 4939264 | tf_op jit(solution)/shard_map/while/body/eval_jaxpr/qhd,nhd->qhn/dot_general | solution.py:51
  133.8 3.4 %fusion.54 = f32[192,10]{0,1:T(8,128)S(1)} fusion(f32[10,512,192]{1,2,0:T(8,128)} %get-tuple-element.257, f32[192,10]{0,1:T(8,128)S(1)} %select_maximum_fusion.2, pred[192,512]{1,0:T(8,128)(4,1)S(1)} %bitcast.76), kind=kLoop, calls=%fused_computation.3.clone.1 | loop fusion | flops 4913280 | bytes 4045824 | tf_op jit(solution)/shard_map/while/body/eval_jaxpr/reduce_sum | solution.py:56
  137.2 0.3 copy.15
  137.4 3.3 %fusion.56 = f32[192,10,64]{0,2,1:T(8,128)S(1)} fusion(bf16[512,10,64]{0,2,1:T(8,128)(2,1)S(1)} %bitcast.78, f32[10,512,192]{1,2,0:T(8,128)} %get-tuple-element.257, f32[192,10]{0,1:T(8,128)S(1)} %select_maximum_fusion.2, pred[192,512]{1,0:T(8,128)(4,1)S(1)} %bitcast.77, f32[192,10,64]{0,2,1:T(8,128)S(1)} %bitcast.82, ...), kind=kOutput, calls=%fused_computation.8.clone.1 | convolution fusion | flops 130990080 | bytes 5684224 | tf_op jit(solution)/shard_map/while/body/eval_jaxpr/qhn,nhd->qhd/dot_general | solution.py:57
  140.8 0.8 copy-done.2
  141.6 0.6 dynamic_slice.28
  142.2 0.6 add_select_fusion.2
  142.7 0.3 fusion.52
  143.1 1.4 constant_dynamic-slice_fusion.3
  144.5 0.3 copy.16
  144.8 3.8 %fusion.53 = (f32[192,10]{0,1:T(8,128)S(1)}, f32[10,512,192]{1,2,0:T(8,128)}) fusion(pred[192,512]{1,0:T(8,128)(4,1)S(1)} %bitcast.75, bf16[512,10,64]{0,2,1:T(8,128)(2,1)S(1)} %bitcast.74, bf16[192,10,64]{0,2,1:T(8,128)(2,1)} %bitcast.79), kind=kOutput, calls=%fused_computation.2.clone.1 | convolution fusion | flops 128776320 | bytes 4939264 | tf_op jit(solution)/shard_map/while/body/eval_jaxpr/qhd,nhd->qhn/dot_general | solution.py:51
  148.5 3.4 %fusion.54 = f32[192,10]{0,1:T(8,128)S(1)} fusion(f32[10,512,192]{1,2,0:T(8,128)} %get-tuple-element.257, f32[192,10]{0,1:T(8,128)S(1)} %select_maximum_fusion.2, pred[192,512]{1,0:T(8,128)(4,1)S(1)} %bitcast.76), kind=kLoop, calls=%fused_computation.3.clone.1 | loop fusion | flops 4913280 | bytes 4045824 | tf_op jit(solution)/shard_map/while/body/eval_jaxpr/reduce_sum | solution.py:56
  151.9 0.3 copy.15
  152.2 3.3 %fusion.56 = f32[192,10,64]{0,2,1:T(8,128)S(1)} fusion(bf16[512,10,64]{0,2,1:T(8,128)(2,1)S(1)} %bitcast.78, f32[10,512,192]{1,2,0:T(8,128)} %get-tuple-element.257, f32[192,10]{0,1:T(8,128)S(1)} %select_maximum_fusion.2, pred[192,512]{1,0:T(8,128)(4,1)S(1)} %bitcast.77, f32[192,10,64]{0,2,1:T(8,128)S(1)} %bitcast.82, ...), kind=kOutput, calls=%fused_computation.8.clone.1 | convolution fusion | flops 130990080 | bytes 5684224 | tf_op jit(solution)/shard_map/while/body/eval_jaxpr/qhn,nhd->qhd/dot_general | solution.py:57
  155.5 0.8 copy-done.2
  156.4 0.6 dynamic_slice.28
  156.9 0.6 add_select_fusion.2
  157.5 0.3 fusion.52
  157.8 1.4 constant_dynamic-slice_fusion.3
  159.2 0.3 copy.16
  159.5 3.8 %fusion.53 = (f32[192,10]{0,1:T(8,128)S(1)}, f32[10,512,192]{1,2,0:T(8,128)}) fusion(pred[192,512]{1,0:T(8,128)(4,1)S(1)} %bitcast.75, bf16[512,10,64]{0,2,1:T(8,128)(2,1)S(1)} %bitcast.74, bf16[192,10,64]{0,2,1:T(8,128)(2,1)} %bitcast.79), kind=kOutput, calls=%fused_computation.2.clone.1 | convolution fusion | flops 128776320 | bytes 4939264 | tf_op jit(solution)/shard_map/while/body/eval_jaxpr/qhd,nhd->qhn/dot_general | solution.py:51
  163.3 3.4 %fusion.54 = f32[192,10]{0,1:T(8,128)S(1)} fusion(f32[10,512,192]{1,2,0:T(8,128)} %get-tuple-element.257, f32[192,10]{0,1:T(8,128)S(1)} %select_maximum_fusion.2, pred[192,512]{1,0:T(8,128)(4,1)S(1)} %bitcast.76), kind=kLoop, calls=%fused_computation.3.clone.1 | loop fusion | flops 4913280 | bytes 4045824 | tf_op jit(solution)/shard_map/while/body/eval_jaxpr/reduce_sum | solution.py:56
  166.9 3.3 %fusion.56 = f32[192,10,64]{0,2,1:T(8,128)S(1)} fusion(bf16[512,10,64]{0,2,1:T(8,128)(2,1)S(1)} %bitcast.78, f32[10,512,192]{1,2,0:T(8,128)} %get-tuple-element.257, f32[192,10]{0,1:T(8,128)S(1)} %select_maximum_fusion.2, pred[192,512]{1,0:T(8,128)(4,1)S(1)} %bitcast.77, f32[192,10,64]{0,2,1:T(8,128)S(1)} %bitcast.82, ...), kind=kOutput, calls=%fused_computation.8.clone.1 | convolution fusion | flops 130990080 | bytes 5684224 | tf_op jit(solution)/shard_map/while/body/eval_jaxpr/qhn,nhd->qhd/dot_general | solution.py:57
  170.3 0.8 copy-done.2
  171.1 0.6 dynamic_slice.28
  171.6 0.6 add_select_fusion.2
  172.2 0.3 fusion.52
  172.6 1.4 constant_dynamic-slice_fusion.3
  174.2 3.8 %fusion.53 = (f32[192,10]{0,1:T(8,128)S(1)}, f32[10,512,192]{1,2,0:T(8,128)}) fusion(pred[192,512]{1,0:T(8,128)(4,1)S(1)} %bitcast.75, bf16[512,10,64]{0,2,1:T(8,128)(2,1)S(1)} %bitcast.74, bf16[192,10,64]{0,2,1:T(8,128)(2,1)} %bitcast.79), kind=kOutput, calls=%fused_computation.2.clone.1 | convolution fusion | flops 128776320 | bytes 4939264 | tf_op jit(solution)/shard_map/while/body/eval_jaxpr/qhd,nhd->qhn/dot_general | solution.py:51
  178.0 3.4 %fusion.54 = f32[192,10]{0,1:T(8,128)S(1)} fusion(f32[10,512,192]{1,2,0:T(8,128)} %get-tuple-element.257, f32[192,10]{0,1:T(8,128)S(1)} %select_maximum_fusion.2, pred[192,512]{1,0:T(8,128)(4,1)S(1)} %bitcast.76), kind=kLoop, calls=%fused_computation.3.clone.1 | loop fusion | flops 4913280 | bytes 4045824 | tf_op jit(solution)/shard_map/while/body/eval_jaxpr/reduce_sum | solution.py:56
  181.7 3.3 %fusion.56 = f32[192,10,64]{0,2,1:T(8,128)S(1)} fusion(bf16[512,10,64]{0,2,1:T(8,128)(2,1)S(1)} %bitcast.78, f32[10,512,192]{1,2,0:T(8,128)} %get-tuple-element.257, f32[192,10]{0,1:T(8,128)S(1)} %select_maximum_fusion.2, pred[192,512]{1,0:T(8,128)(4,1)S(1)} %bitcast.77, f32[192,10,64]{0,2,1:T(8,128)S(1)} %bitcast.82, ...), kind=kOutput, calls=%fused_computation.8.clone.1 | convolution fusion | flops 130990080 | bytes 5684224 | tf_op jit(solution)/shard_map/while/body/eval_jaxpr/qhn,nhd->qhd/dot_general | solution.py:57
  185.0 0.8 copy-done.2
  185.8 0.6 dynamic_slice.28
  186.4 0.6 add_select_fusion.2
  186.9 0.3 fusion.52
  187.3 1.4 constant_dynamic-slice_fusion.3
  189.0 3.8 %fusion.53 = (f32[192,10]{0,1:T(8,128)S(1)}, f32[10,512,192]{1,2,0:T(8,128)}) fusion(pred[192,512]{1,0:T(8,128)(4,1)S(1)} %bitcast.75, bf16[512,10,64]{0,2,1:T(8,128)(2,1)S(1)} %bitcast.74, bf16[192,10,64]{0,2,1:T(8,128)(2,1)} %bitcast.79), kind=kOutput, calls=%fused_computation.2.clone.1 | convolution fusion | flops 128776320 | bytes 4939264 | tf_op jit(solution)/shard_map/while/body/eval_jaxpr/qhd,nhd->qhn/dot_general | solution.py:51
  192.8 3.4 %fusion.54 = f32[192,10]{0,1:T(8,128)S(1)} fusion(f32[10,512,192]{1,2,0:T(8,128)} %get-tuple-element.257, f32[192,10]{0,1:T(8,128)S(1)} %select_maximum_fusion.2, pred[192,512]{1,0:T(8,128)(4,1)S(1)} %bitcast.76), kind=kLoop, calls=%fused_computation.3.clone.1 | loop fusion | flops 4913280 | bytes 4045824 | tf_op jit(solution)/shard_map/while/body/eval_jaxpr/reduce_sum | solution.py:56
  196.4 3.3 %fusion.56 = f32[192,10,64]{0,2,1:T(8,128)S(1)} fusion(bf16[512,10,64]{0,2,1:T(8,128)(2,1)S(1)} %bitcast.78, f32[10,512,192]{1,2,0:T(8,128)} %get-tuple-element.257, f32[192,10]{0,1:T(8,128)S(1)} %select_maximum_fusion.2, pred[192,512]{1,0:T(8,128)(4,1)S(1)} %bitcast.77, f32[192,10,64]{0,2,1:T(8,128)S(1)} %bitcast.82, ...), kind=kOutput, calls=%fused_computation.8.clone.1 | convolution fusion | flops 130990080 | bytes 5684224 | tf_op jit(solution)/shard_map/while/body/eval_jaxpr/qhn,nhd->qhd/dot_general | solution.py:57
  199.8 0.8 copy-done.2
  200.6 1.1 fusion.21
  201.7 1.3 convolution_convert_fusion
  (58 shorter events, 2.4 us)
Async XLA Ops:
  6.5 195.2 %copy-start = (bf16[640,1024]{1,0:T(8,128)(2,1)S(1)}, bf16[640,1024]{1,0:T(8,128)(2,1)}, u32[]{:S(2)}) copy-start(bf16[640,1024]{1,0:T(8,128)(2,1)} %param.11) | copy-start | bytes 3932164
  6.5 54.6 %all-gather.3.cloned.1.call-start = ((), (), s32[]{:S(2)}) async-start(), calls=%async_computation | async-start | bytes 4177920 | tf_op jit(solution)/shard_map/all_gather | solution.py:111
  7.3 104.0 %all-gather.5.cloned.1.call-start = ((), (), s32[]{:S(2)}) async-start(), calls=%async_computation.1 | async-start | bytes 4177920 | tf_op jit(solution)/shard_map/all_gather | solution.py:112
  119.0 3.7 %copy-start.1 = (f32[192,640]{0,1:T(8,128)S(1)}, f32[192,640]{0,1:T(8,128)}, u32[]{:S(2)}) copy-start(f32[192,640]{0,1:T(8,128)} %get-tuple-element.273) | copy-start | bytes 1474564 | tf_op jit(solution)/shard_map/while
  126.0 0.8 copy-start.2
  133.8 3.7 %copy-start.1 = (f32[192,640]{0,1:T(8,128)S(1)}, f32[192,640]{0,1:T(8,128)}, u32[]{:S(2)}) copy-start(f32[192,640]{0,1:T(8,128)} %get-tuple-element.273) | copy-start | bytes 1474564 | tf_op jit(solution)/shard_map/while
  140.8 0.8 copy-start.2
  148.5 3.7 %copy-start.1 = (f32[192,640]{0,1:T(8,128)S(1)}, f32[192,640]{0,1:T(8,128)}, u32[]{:S(2)}) copy-start(f32[192,640]{0,1:T(8,128)} %get-tuple-element.273) | copy-start | bytes 1474564 | tf_op jit(solution)/shard_map/while
  155.5 0.8 copy-start.2
  163.3 3.7 %copy-start.1 = (f32[192,640]{0,1:T(8,128)S(1)}, f32[192,640]{0,1:T(8,128)}, u32[]{:S(2)}) copy-start(f32[192,640]{0,1:T(8,128)} %get-tuple-element.273) | copy-start | bytes 1474564 | tf_op jit(solution)/shard_map/while
  170.2 0.8 copy-start.2
  178.0 3.7 %copy-start.1 = (f32[192,640]{0,1:T(8,128)S(1)}, f32[192,640]{0,1:T(8,128)}, u32[]{:S(2)}) copy-start(f32[192,640]{0,1:T(8,128)} %get-tuple-element.273) | copy-start | bytes 1474564 | tf_op jit(solution)/shard_map/while
  185.0 0.8 copy-start.2
  192.7 3.7 %copy-start.1 = (f32[192,640]{0,1:T(8,128)S(1)}, f32[192,640]{0,1:T(8,128)}, u32[]{:S(2)}) copy-start(f32[192,640]{0,1:T(8,128)} %get-tuple-element.273) | copy-start | bytes 1474564 | tf_op jit(solution)/shard_map/while
  199.7 0.8 copy-start.2
Sparse Core Ops, SparseCore 0:
  9.6 51.4 all-gather.2
  63.3 47.8 all-gather.4
where the time goes:
time: 211 us; the launch traced here: 210 us
  waiting for transfers between devices  101 us (48%)
  matrix products  47.7 us (23%)
  other arithmetic  24.7 us (12%)
  local copies, waits for them, and re-layouts  22.8 us (11%)
  between operations  13.5 us (6%)
    all_gather x1, waiting for transfers between devices, body(): lax.all_gather(values, ('arc', 'blk'), axis=0, tiled=True)  50.1 us
    all_gather x1, waiting for transfers between devices, body(): lax.all_gather(keys, ('arc', 'blk'), axis=0, tiled=True)  49.1 us
    dot_general x6, matrix products, attend_slice(): jnp.einsum('qhd,nhd->qhn', q3, k3, preferred_element_type=jnp.float32)  22.6 us
    reduce_sum x6, other arithmetic, attend_slice(): total = total * factor + jnp.sum(probs, axis=-1)  20.2 us
    dot_general x6, matrix products, attend_slice(): jnp.einsum('qhn,nhd->qhd', probs.astype(jnp.bfloat16), v3, preferred_elem...  19.9 us
    dynamic_slice x24, local copies, waits for them, and re-layouts, fold(): result, _ = lax.scan(inner, state, (kslices, vslices, offsets))  14.8 us
    while x30, local copies, waits for them, and re-layouts  5 us
  transfers between devices with their start and end apart: 2, of which 2 were waited for; matrix products, arithmetic and copies ran while one was open for 2% of the time, Pallas kernels for 0%

commit v1 on v0

v1 whole, which is shorter than its diff:
```python
import functools

import jax
import jax.numpy as jnp
from jax import lax
from jax.experimental import pallas as pl
from jax.experimental.pallas import tpu as pltpu
from jax.sharding import PartitionSpec as P

HEADS = 10
HD = 64
BLOCK = 32
PAIRS = HEADS // 2
LANES = 128
NEG = -1e30
MESH = pl.DeviceIdType.MESH
UP, DOWN, SIDE, CORE = 0, 1, 2, 3


def dot(a, b, ca, cb):
    return lax.dot_general(a, b, (((ca,), (cb,)), ((), ())), preferred_element_type=jnp.float32)


def iota(shape, dim):
    return lax.broadcasted_iota(jnp.int32, shape, dim)


def kernel(
    nz, ny, q_ref, k_ref, v_ref, w_ref, covis_ref, view_ref, o_ref,
    buf, qaug, acc, top, visq, send, recv, local,
):
    tok = q_ref.shape[0]
    per = tok // BLOCK
    count = covis_ref.shape[0]
    n_blk = nz * ny
    c = lax.axis_index("arc")
    b = lax.axis_index("blk")
    z = b // ny
    y = b % ny
    has_up = z < nz - 1
    has_down = z > 0
    mate = z + 1 - 2 * (z % 2)
    below, above = z, nz - 1 - z
    short = jnp.minimum(below, above)

    def order(i):
        step = (i + 1) // 2
        near = jnp.where(i % 2 == 1, z - step, z + step)
        far = jnp.where(above > below, z + (i - short), z - (i - short))
        return jnp.where(i <= 2 * short, near, far)

    def target(way):
        if way == UP:
            return {"blk": b + ny}
        if way == DOWN:
            return {"blk": b - ny}
        if way == SIDE:
            return {"blk": z * ny + (1 - y)}
        return {"arc": 1 - c}

    def place(piece, blk, core):
        return buf.at[piece, blk, pl.ds(pl.multiple_of(core * tok, 16), tok), :]

    def copy(way, piece, blk, src=None):
        dst = place(piece, blk, c)
        return pltpu.make_async_remote_copy(
            src_ref=dst if src is None else src,
            dst_ref=dst,
            send_sem=send.at[way, piece, blk],
            recv_sem=recv.at[piece, blk, c],
            device_id=target(way),
            device_id_type=MESH,
        )

    def arrive(piece, blk, core):
        dst = place(piece, blk, core)
        pltpu.make_async_remote_copy(
            src_ref=dst,
            dst_ref=dst,
            send_sem=send.at[CORE, piece, blk],
            recv_sem=recv.at[piece, blk, core],
            device_id=target(CORE),
            device_id_type=MESH,
        ).wait_recv()

    def along(piece, z0, act):
        blk = z0 * ny + y

        @pl.when((z0 <= z) & has_up)
        def _():
            act(copy(UP, piece, blk, None))

        @pl.when((z0 >= z) & has_down)
        def _():
            act(copy(DOWN, piece, blk, None))

        @pl.when(jnp.logical_or(piece == 0, z0 != mate))
        def _():
            act(copy(SIDE, piece, blk, None))

        act(copy(CORE, piece, blk, None))

    def across(piece, z0, act):
        blk = z0 * ny + (1 - y)
        if piece == 1:

            @pl.when((z0 == z) & (mate > z))
            def _():
                act(copy(UP, piece, blk))

            @pl.when((z0 == z) & (mate < z))
            def _():
                act(copy(DOWN, piece, blk))

        act(copy(CORE, piece, blk))

    def start(d):
        d.start()

    def done(d):
        d.wait_send()

    mine = [
        pltpu.make_async_copy(ref, place(piece, b, c), local.at[piece])
        for piece, ref in enumerate((k_ref, v_ref))
    ]
    for d in mine:
        d.start()

    barrier = pltpu.get_barrier_semaphore()

    @pl.when(has_up)
    def _():
        pl.semaphore_signal(barrier, inc=1, device_id=target(UP), device_id_type=MESH)

    @pl.when(has_down)
    def _():
        pl.semaphore_signal(barrier, inc=1, device_id=target(DOWN), device_id_type=MESH)

    pl.semaphore_signal(barrier, inc=1, device_id=target(SIDE), device_id_type=MESH)
    pl.semaphore_signal(barrier, inc=1, device_id=target(CORE), device_id_type=MESH)
    pl.semaphore_wait(barrier, 2 + has_up.astype(jnp.int32) + has_down.astype(jnp.int32))

    for piece in range(2):
        mine[piece].wait()
        along(piece, z, start)

    views = jnp.where(iota((count, count), 0) == view_ref[...], 1.0, 0.0).astype(jnp.bfloat16)
    seen = covis_ref[...].astype(jnp.float32).astype(jnp.bfloat16)
    half = dot(seen, views, 1, 0).astype(jnp.bfloat16)
    vis = dot(views, half, 0, 0).astype(jnp.bfloat16)
    first = (c * n_blk + b) * per
    own = (iota((count, LANES), 0) - first == iota((count, LANES), 1)) & (
        iota((count, LANES), 1) < per
    )
    visq[...] = dot(vis, jnp.where(own, 1.0, 0.0).astype(jnp.bfloat16), 0, 0).astype(jnp.bfloat16)

    left = iota((tok, LANES), 1) < HD
    onehot = jnp.where(iota((tok, LANES), 0) // BLOCK == iota((tok, LANES), 1), 1.0, 0.0)
    onehot = onehot.astype(jnp.bfloat16)
    for p in range(PAIRS):
        q = q_ref[:, p * LANES:(p + 1) * LANES].astype(jnp.float32) * HD ** (-0.5)
        qaug[p, :tok, :LANES] = jnp.where(left, q, 0.0).astype(jnp.bfloat16)
        qaug[p, tok:, :LANES] = jnp.where(left, 0.0, q).astype(jnp.bfloat16)
        qaug[p, :tok, LANES:] = onehot
        qaug[p, tok:, LANES:] = onehot
    acc[...] = jnp.zeros_like(acc)
    top[...] = jnp.full(top.shape, NEG, jnp.float32)

    def attend(blk):
        rows = 2 * tok
        r = iota((rows, count), 0)
        core = (r >= tok).astype(jnp.int32)
        slot = (core * n_blk + blk) * per + (r - core * tok) // BLOCK
        spread = jnp.where(slot == iota((rows, count), 1), 1.0, 0.0).astype(jnp.bfloat16)
        bias = ((1.0 - dot(spread, visq[...], 1, 0)) * NEG).astype(jnp.bfloat16)
        ones = jnp.ones((rows, LANES), jnp.bfloat16)
        for p in range(PAIRS):
            cols = slice(p * LANES, (p + 1) * LANES)
            keys = jnp.concatenate([buf[0, blk, :, cols], bias], axis=1)
            scores = dot(keys, qaug[p], 1, 1)
            before = top[p]
            fresh = jnp.maximum(before, jnp.max(scores, axis=0, keepdims=True))
            probs = jnp.exp(scores - fresh[:1]).astype(jnp.bfloat16)
            factor = jnp.exp(before - fresh)
            values = jnp.concatenate([buf[1, blk, :, cols], ones], axis=1)
            mixed = dot(values, probs, 0, 0)
            acc[p] = acc[p] * factor[:1] + mixed[:LANES + 8]
            top[p] = fresh

    def chunk(blk):
        arrive(0, blk, 1 - c)
        arrive(1, blk, 1 - c)
        attend(blk)

    chunk(b)

    def step(i, carry):
        z0, z1 = order(i), order(i - 1)
        for piece in range(2):
            arrive(piece, z0 * ny + y, c)
            along(piece, z0, start)
            arrive(piece, z1 * ny + (1 - y), c)
            across(piece, z1, start)
        chunk(z0 * ny + y)
        chunk(z1 * ny + (1 - y))
        return carry

    lax.fori_loop(1, nz, step, 0)
    last = order(nz - 1)
    for piece in range(2):
        arrive(piece, last * ny + (1 - y), c)
        across(piece, last, start)
    chunk(last * ny + (1 - y))

    parts = []
    for p in range(PAIRS):
        flat = (acc[p, :LANES] * (1.0 / acc[p, LANES:LANES + 1])).T
        parts.append(jnp.where(left, flat[:tok], flat[tok:]).astype(jnp.bfloat16))
    attn = jnp.concatenate(parts, axis=1)
    o_ref[...] = dot(attn, w_ref[...], 1, 0).astype(jnp.bfloat16)

    def drain(i, carry):
        for piece in range(2):
            along(piece, order(i), done)
            across(piece, order(i), done)
        return carry

    lax.fori_loop(0, nz, drain, 0)


def body(nz, ny, queries, keys, values, out_weight, covis, block_view):
    tok, width = queries.shape
    model = out_weight.shape[1]
    n_blk = nz * ny
    vmem = pl.BlockSpec(memory_space=pltpu.VMEM)
    hbm = pl.BlockSpec(memory_space=pl.ANY)
    return pl.pallas_call(
        functools.partial(kernel, nz, ny),
        out_shape=jax.ShapeDtypeStruct((tok, model), jnp.bfloat16),
        in_specs=[vmem, hbm, hbm, vmem, vmem, vmem],
        out_specs=vmem,
        scratch_shapes=[
            pltpu.VMEM((2, n_blk, 2 * tok, width), jnp.bfloat16),
            pltpu.VMEM((PAIRS, 2 * tok, 2 * LANES), jnp.bfloat16),
            pltpu.VMEM((PAIRS, LANES + 8, 2 * tok), jnp.float32),
            pltpu.VMEM((PAIRS, 8, 2 * tok), jnp.float32),
            pltpu.VMEM((covis.shape[0], LANES), jnp.bfloat16),
            pltpu.SemaphoreType.DMA((4, 2, n_blk)),
            pltpu.SemaphoreType.DMA((2, n_blk, 2)),
            pltpu.SemaphoreType.DMA((2,)),
        ],
        compiler_params=pltpu.CompilerParams(
            collective_id=0, has_side_effects=True, vmem_limit_bytes=56 * 2**20
        ),
    )(queries, keys, values, out_weight, covis, block_view[None, :])


def solution(mesh):
    ny = 2
    nz = mesh.shape["blk"] // ny
    return jax.shard_map(
        functools.partial(body, nz, ny),
        mesh=mesh,
        in_specs=(
            P(("groups", "arc", "blk"), None),
            P(("groups", "arc", "blk"), None),
            P(("groups", "arc", "blk"), None),
            P(),
            P("groups", None),
            P("groups"),
        ),
        out_specs=P(("groups", "arc", "blk"), None),
        check_vma=False,
    )
```

time: 211 us -> 62.2 us (0.29)
  waiting for transfers between devices: 101 us -> 0 us
  Pallas kernels: 0 us -> 60.3 us
  matrix products: 47.7 us -> 0 us
  other arithmetic: 24.7 us -> 0 us
  local copies, waits for them, and re-layouts: 22.8 us -> 1.77 us
  between operations: 13.5 us -> 0.01 us
    all_gather x2 -> x0, waiting for transfers between devices: 99.2 us -> none  [the longest x1 50.1 us: body(): lax.all_gather(values, ('arc', 'blk'), axis=0, tiled=True)]
    pallas_call x0 -> x1, Pallas kernels: none -> 60.3 us  [body(): pl.pallas_call(functools.partial(kernel, nz, ny), out_shape=jax.ShapeDtyp...]
    dot_general x22 -> x0, matrix products: 47.7 us -> none  [the longest x6 22.6 us: attend_slice(): jnp.einsum('qhd,nhd->qhn', q3, k3, preferred_element_type=jnp.float32)]
    reduce_sum x6 -> x0, other arithmetic: 20.2 us -> none  [attend_slice(): total = total * factor + jnp.sum(probs, axis=-1)]
    dynamic_slice x24 -> x0, local copies, waits for them, and re-layouts: 14.8 us -> none  [fold(): result, _ = lax.scan(inner, state, (kslices, vslices, offsets))]
    while x30 -> x0, local copies, waits for them, and re-layouts: 5 us -> none
    select_n x6 -> x0, other arithmetic: 3.33 us -> none  [seen_blocks(): kblock = (offset + jnp.arange(length, dtype=jnp.int32)) // BLOCK]
  transfers between devices with their start and end apart: 2 -> 0, of which waited for: 2 -> 0; matrix products, arithmetic and copies ran while one was open for 2% -> 0% of each run, Pallas kernels for 0% -> 0%
where the time goes in v1:
time: 62.2 us; the launch traced here: 62 us
  Pallas kernels  60.3 us (97%)
  local copies, waits for them, and re-layouts  1.77 us (3%)
    pallas_call x1, Pallas kernels, body(): pl.pallas_call(functools.partial(kernel, nz, ny), out_shape=jax.ShapeDtyp...  60.3 us
    unnamed x1, local copies, waits for them, and re-layouts  1.77 us

profile of v1, /device:TPU:0, one launch (start us, length us, event | category | flops | bytes accessed | tf_op | source)
XLA Modules:
  0.0 62.0 jit_solution(12062015152555362770)
XLA Ops:
  0.0 60.3 %shard_map.64 = bf16[192,1024]{1,0:T(8,128)(2,1)} custom-call(bf16[192,640]{1,0:T(8,128)(2,1)} %q_ref.1, bf16[192,640]{1,0:T(8,128)(2,1)} %k_ref.1, bf16[192,640]{1,0:T(8,128)(2,1)} %v_ref.1, bf16[640,1024]{1,0:T(8,128)(2,1)} %w_ref.1, s32[96,96]{1,0:T(8,128)} %covis_ref.1, s32[1,96]{1,0:T(1,128)} %bitcast.1), custom_call_target="tpu_custom_call" | custom-call | tf_op jit(solution)/shard_map/pallas_call | solution.py:238
  60.3 1.8 %copy.8 = bf16[192,1024]{1,0:T(8,128)(2,1)} copy(bf16[192,1024]{1,0:T(8,128)(2,1)} %shard_map.64) | data formatting | bytes 786432

commit v2 on v1

--- a/solution.py
+++ b/solution.py
@@ -26,7 +26,7 @@
 
 
 def kernel(
-    nz, ny, q_ref, k_ref, v_ref, w_ref, covis_ref, view_ref, o_ref,
+    nz, ny, q_ref, k_ref, v_ref, covis_ref, view_ref, o_ref,
     buf, qaug, acc, top, visq, send, recv, local,
 ):
     tok = q_ref.shape[0]
@@ -39,14 +39,15 @@
     y = b % ny
     has_up = z < nz - 1
     has_down = z > 0
-    mate = z + 1 - 2 * (z % 2)
+    inner = has_up & has_down
     below, above = z, nz - 1 - z
     short = jnp.minimum(below, above)
+    toward = jnp.where(below <= above, -1, 1)
 
     def order(i):
         step = (i + 1) // 2
-        near = jnp.where(i % 2 == 1, z - step, z + step)
-        far = jnp.where(above > below, z + (i - short), z - (i - short))
+        near = jnp.where(i % 2 == 1, z + toward * step, z - toward * step)
+        far = z - toward * (i - short)
         return jnp.where(i <= 2 * short, near, far)
 
     def target(way):
@@ -94,9 +95,13 @@
         def _():
             act(copy(DOWN, piece, blk, None))
 
-        @pl.when(jnp.logical_or(piece == 0, z0 != mate))
-        def _():
-            act(copy(SIDE, piece, blk, None))
+        if piece == 0:
+            act(copy(SIDE, piece, blk))
+        else:
+
+            @pl.when((z0 == z) | ((z0 > 0) & (z0 < nz - 1)))
+            def _():
+                act(copy(SIDE, piece, blk))
 
         act(copy(CORE, piece, blk, None))
 
@@ -104,11 +109,11 @@
         blk = z0 * ny + (1 - y)
         if piece == 1:
 
-            @pl.when((z0 == z) & (mate > z))
+            @pl.when((z0 == 0) & has_up)
             def _():
                 act(copy(UP, piece, blk))
 
-            @pl.when((z0 == z) & (mate < z))
+            @pl.when((z0 == nz - 1) & has_down)
             def _():
                 act(copy(DOWN, piece, blk))
 
@@ -195,30 +200,48 @@
 
     chunk(b)
 
+    def near_events(i):
+        for piece in range(2):
+            arrive(piece, order(i) * ny + y, c)
+            along(piece, order(i), start)
+
+    def side_event(piece, i):
+        arrive(piece, order(i) * ny + (1 - y), c)
+        across(piece, order(i), start)
+
     def step(i, carry):
-        z0, z1 = order(i), order(i - 1)
-        for piece in range(2):
-            arrive(piece, z0 * ny + y, c)
-            along(piece, z0, start)
-            arrive(piece, z1 * ny + (1 - y), c)
-            across(piece, z1, start)
-        chunk(z0 * ny + y)
-        chunk(z1 * ny + (1 - y))
+        near_events(i)
+        side_event(0, i - 1)
+        side_event(1, i - 1)
+        chunk(order(i) * ny + y)
+        chunk(order(i - 1) * ny + (1 - y))
         return carry
 
-    lax.fori_loop(1, nz, step, 0)
-    last = order(nz - 1)
-    for piece in range(2):
-        arrive(piece, last * ny + (1 - y), c)
-        across(piece, last, start)
-    chunk(last * ny + (1 - y))
+    lax.fori_loop(1, nz - 1, step, 0)
+    last = nz - 1
+    near_events(last)
+    side_event(0, last - 1)
+    side_event(1, last - 1)
+
+    @pl.when(inner)
+    def _():
+        side_event(1, last)
+
+    chunk(order(last) * ny + y)
+    chunk(order(last - 1) * ny + (1 - y))
+    side_event(0, last)
+
+    @pl.when(jnp.logical_not(inner))
+    def _():
+        side_event(1, last)
+
+    chunk(order(last) * ny + (1 - y))
 
     parts = []
     for p in range(PAIRS):
         flat = (acc[p, :LANES] * (1.0 / acc[p, LANES:LANES + 1])).T
         parts.append(jnp.where(left, flat[:tok], flat[tok:]).astype(jnp.bfloat16))
-    attn = jnp.concatenate(parts, axis=1)
-    o_ref[...] = dot(attn, w_ref[...], 1, 0).astype(jnp.bfloat16)
+    o_ref[...] = jnp.concatenate(parts, axis=1)
 
     def drain(i, carry):
         for piece in range(2):
@@ -231,14 +254,13 @@
 
 def body(nz, ny, queries, keys, values, out_weight, covis, block_view):
     tok, width = queries.shape
-    model = out_weight.shape[1]
     n_blk = nz * ny
     vmem = pl.BlockSpec(memory_space=pltpu.VMEM)
     hbm = pl.BlockSpec(memory_space=pl.ANY)
-    return pl.pallas_call(
+    attn = pl.pallas_call(
         functools.partial(kernel, nz, ny),
-        out_shape=jax.ShapeDtypeStruct((tok, model), jnp.bfloat16),
-        in_specs=[vmem, hbm, hbm, vmem, vmem, vmem],
+        out_shape=jax.ShapeDtypeStruct((tok, width), jnp.bfloat16),
+        in_specs=[vmem, hbm, hbm, vmem, vmem],
         out_specs=vmem,
         scratch_shapes=[
             pltpu.VMEM((2, n_blk, 2 * tok, width), jnp.bfloat16),
@@ -253,7 +275,8 @@
         compiler_params=pltpu.CompilerParams(
             collective_id=0, has_side_effects=True, vmem_limit_bytes=56 * 2**20
         ),
-    )(queries, keys, values, out_weight, covis, block_view[None, :])
+    )(queries, keys, values, covis, block_view[None, :])
+    return jnp.dot(attn, out_weight, preferred_element_type=jnp.float32).astype(jnp.bfloat16)
 
 
 def solution(mesh):

time: 62.2 us -> 61.6 us (level)
  matrix products: 0 us -> 2.17 us
  local copies, waits for them, and re-layouts: 1.77 us -> 0.01 us
  Pallas kernels: 60.3 us -> 59.2 us
    dot_general x0 -> x1, matrix products: none -> 2.17 us  [body(): jnp.dot(attn, out_weight, preferred_element_type=jnp.float32)]
    unnamed x1 -> x2, local copies, waits for them, and re-layouts: 1.77 us -> 0.01 us
    pallas_call x1, Pallas kernels: 60.3 us -> 59.2 us  [body(): pl.pallas_call(functools.partial(kernel, nz, ny), out_shape=jax.ShapeDtyp...]
where the time goes in v2:
time: 61.6 us; the launch traced here: 61.4 us
  Pallas kernels  59.2 us (96%)
  matrix products  2.17 us (4%)
    pallas_call x1, Pallas kernels, body(): pl.pallas_call(functools.partial(kernel, nz, ny), out_shape=jax.ShapeDtyp...  59.2 us
    dot_general x1, matrix products, body(): jnp.dot(attn, out_weight, preferred_element_type=jnp.float32)  2.17 us

profile of v2, /device:TPU:0, one launch (start us, length us, event | category | flops | bytes accessed | tf_op | source)
XLA Modules:
  0.0 61.4 jit_solution(315101311471681945)
XLA Ops:
  0.0 0.0 copy-start
  0.0 59.2 %shard_map.64 = bf16[192,640]{1,0:T(8,128)(2,1)} custom-call(bf16[192,640]{1,0:T(8,128)(2,1)} %q_ref.1, bf16[192,640]{1,0:T(8,128)(2,1)} %k_ref.1, bf16[192,640]{1,0:T(8,128)(2,1)} %v_ref.1, s32[96,96]{1,0:T(8,128)} %covis_ref.1, s32[1,96]{1,0:T(1,128)} %bitcast.3), custom_call_target="tpu_custom_call" | custom-call | tf_op jit(solution)/shard_map/pallas_call | solution.py:260
  59.2 0.0 copy-done
  59.2 2.2 %convolution_convert_fusion = bf16[192,1024]{1,0:T(8,128)(2,1)} fusion(bf16[192,640]{1,0:T(8,128)(2,1)} %shard_map.64, bf16[640,1024]{1,0:T(8,128)(2,1)S(1)} %copy-done), kind=kOutput, calls=%fused_computation | convolution fusion | flops 251854848 | bytes 1949696 | tf_op jit(solution)/shard_map/dot_general | solution.py:279
Async XLA Ops:
  0.0 59.2 %copy-start = (bf16[640,1024]{1,0:T(8,128)(2,1)S(1)}, bf16[640,1024]{1,0:T(8,128)(2,1)}, u32[]{:S(2)}) copy-start(bf16[640,1024]{1,0:T(8,128)(2,1)} %param.9) | copy-start | bytes 3932164
